TPU v7x, 32 devices: a whole 2x2x4 slice. The times are simulated.
32 devices in a mesh: sec: 4 (over y, x), tile: 8 (over z, core).
Axes of the slice: x: 2, y: 2, z: 4, core: 2. Of those that a mesh axis runs over, the one named last changes fastest.
Arguments:
- images: bfloat16 [4, 640, 760], P('sec', 'tile'), may hold values from -30 to 30
- patch_mask: int32 [4, 16, 16], P('sec', 'tile'), may hold values 0 or 1
- springs: int32 [4, 2, 16, 16], P('sec', None, 'tile'), may hold values 0 or 1
- groups: int32 [4], replicated, may hold values from 0 to 1, never falling along the last dimension, each value on 1 to 3 neighbouring positions
Outputs:
- flows: float32 [4, 2, 2, 16, 16], P('sec', None, None, 'tile')
- displacement: float32 [4, 2, 16, 16], P('sec', None, 'tile')
All inputs are finite; a program needn't handle non-finite values. No bound on the sum of `patch_mask` or of `springs` on one device may be relied on, other than what follows from the above.
Results may differ from a plain program's by a relative error of at most 0.012.
The roundings to bfloat16 on the way count: a program that leaves them out, or rounds other values in their place, can miss the bound.
Values may be sent and summed in bfloat16 or wider, within the bound.
A program may use at most 448 MiB of HBM per device.

v0:
```python
import functools
import math

import jax
import jax.numpy as jnp
import numpy as np
from jax import lax
from jax.experimental import pallas as pl
from jax.experimental.pallas import tpu as pltpu
from jax.sharding import PartitionSpec as P

P_SIZE = 160
STRIDE = 40
PR = 2
NC = 16
RELAX = 4
HALF = 80
ABOVE = 48
ROWS = 2 * HALF + ABOVE
FOLD = 96
WIDE = 768
SHIFT = 64
TILES = P_SIZE // 8

spring_stiffness = 1.0
flow_pull = 0.5
step_size = 0.2
sharpness = 25.0


def full_tables():
    indices = np.arange(P_SIZE)
    angle = (indices[:, None] * indices[None, :] % P_SIZE).astype(np.float32) * np.float32(
        2.0 * math.pi / P_SIZE
    )
    exact = angle.astype(np.float64)
    cosine = np.cos(exact).astype(np.float32).astype(jnp.bfloat16).astype(np.float32)
    sine = np.sin(exact).astype(np.float32).astype(jnp.bfloat16).astype(np.float32)
    return cosine, sine


def folded_tables():
    cosine, sine = full_tables()
    kept = HALF + 1
    first = np.zeros((PR, 2, FOLD, ROWS), np.float32)
    for node_row in range(PR):
        rows = slice(node_row * STRIDE, node_row * STRIDE + P_SIZE)
        first[node_row, 0, :kept, rows] = cosine[:kept]
        first[node_row, 1, :kept, rows] = sine[:kept]
    second = np.zeros((8, 256, 256), np.float32)
    for case in range(8):
        offset = STRIDE * case % SHIFT
        second[case, offset : offset + P_SIZE, :kept] = cosine[:, :kept]
        second[case, offset : offset + P_SIZE, 128 : 128 + kept] = sine[:, :kept]
    twice = np.full((kept,), 2.0, np.float32)
    twice[0] = twice[HALF] = 1.0
    third = np.zeros((P_SIZE, 2 * FOLD), np.float32)
    third[:, :kept] = cosine[:, :kept] * twice
    third[:, FOLD : FOLD + kept] = -2.0 * sine[:, :kept]
    fourth = np.zeros((256, P_SIZE), np.float32)
    fourth[:kept] = cosine[:kept] * twice[:, None]
    fourth[128 : 128 + kept] = -2.0 * sine[:kept]
    offsets = (np.arange(P_SIZE) + HALF) % P_SIZE - HALF
    sums = np.zeros((8, P_SIZE), np.float32)
    sums[0] = 1.0
    sums[1] = offsets
    made = [
        table.astype(jnp.bfloat16)
        for table in (first.reshape(PR * 2 * FOLD, ROWS), second, third, fourth)
    ]
    return made + [sums]


def dot(left, right):
    return jnp.dot(left, right, preferred_element_type=jnp.float32)


def phase_section(section, rows, first_ref, wide_ref, phase_ref):
    span = PR * 2 * FOLD
    wide_ref[:, : rows.shape[1]] = dot(first_ref[...], rows)
    whole = wide_ref[...]
    low = section * span
    phase_ref[0, low : low + span] = whole.astype(jnp.bfloat16)
    phase_ref[1, low : low + span] = pltpu.roll(whole, WIDE - SHIFT, 1).astype(jnp.bfloat16)


def column_step(c, second_ref, third_ref, fourth_ref, phase_ref, spec_ref, mix_ref, acc_ref):
    block = STRIDE * c // SHIFT
    start = pl.multiple_of(block // 2 * 128, 128)
    window = phase_ref[block % 2, :, pl.ds(start, 256)]
    spec_ref[...] = dot(window, second_ref[c % 8])
    factor = sharpness / float(P_SIZE) ** 4 * math.log2(math.e)

    def quarters(section, node_row):
        low = (section * PR + node_row) * 2 * FOLD
        return (
            spec_ref[low : low + FOLD, :128],
            spec_ref[low + FOLD : low + 2 * FOLD, 128:],
            spec_ref[low + FOLD : low + 2 * FOLD, :128],
            spec_ref[low : low + FOLD, 128:],
        )

    for node_row in range(PR):
        p, q, u, v = quarters(0, node_row)
        for distance in (1, 2):
            pair = (distance - 1) * PR + node_row
            pp, qq, uu, vv = quarters(distance, node_row)
            mix_ref[pair, :FOLD, :128] = (p * pp + q * qq + u * uu + v * vv).astype(jnp.bfloat16)
            mix_ref[pair, :FOLD, 128:] = (u * qq - v * pp + p * vv - q * uu).astype(jnp.bfloat16)
            mix_ref[pair, FOLD:, :128] = (p * uu - u * pp + v * qq - q * vv).astype(jnp.bfloat16)
            mix_ref[pair, FOLD:, 128:] = (p * qq + q * pp - u * vv - v * uu).astype(jnp.bfloat16)
    for pair in range(2 * PR):
        back = dot(third_ref[...], mix_ref[pair]).astype(jnp.bfloat16)
        raw = dot(back, fourth_ref[...])
        pieces = [raw[8 * i : 8 * i + 8] for i in range(TILES)]
        top = functools.reduce(jnp.maximum, pieces)
        total = jnp.zeros_like(top)
        lean = jnp.zeros_like(top)
        for i, piece in enumerate(pieces):
            weight = jnp.exp2((piece - top) * factor)
            total = total + weight
            base = float(8 * i if 8 * i < HALF else 8 * i - P_SIZE)
            if base:
                lean = lean + base * weight
        acc_ref[0, pair, c] = top
        acc_ref[1, pair, c] = total
        acc_ref[2, pair, c] = lean


def finish_pair(pair, acc_ref, sums_ref):
    factor = sharpness / float(P_SIZE) ** 4 * math.log2(math.e)
    tops = acc_ref[0, pair]
    top = jnp.max(jnp.max(tops, axis=2, keepdims=True), axis=1, keepdims=True)
    scale = jnp.exp2((tops - top) * factor)
    total = acc_ref[1, pair] * scale
    within = lax.broadcasted_iota(jnp.int32, total.shape, 1).astype(jnp.float32)
    lean = acc_ref[2, pair] * scale + within * total
    total = jnp.sum(total, axis=1)
    lean = jnp.sum(lean, axis=1)

    def over_lanes(values):
        return lax.dot_general(
            sums_ref[...],
            values,
            (((1,), (1,)), ((), ())),
            precision=lax.Precision.HIGHEST,
            preferred_element_type=jnp.float32,
        )

    sums = over_lanes(total)
    leans = over_lanes(lean)
    return leans[0:1] / sums[0:1], sums[1:2] / sums[0:1]


def flow_kernel(
    rows_ref, first_ref, second_ref, third_ref, fourth_ref, sums_ref, out_ref,
    wide_ref, phase_ref, spec_ref, mix_ref, acc_ref,
):
    wide_ref[:, WIDE - 128 :] = jnp.zeros((wide_ref.shape[0], 128), jnp.float32)
    for section in range(3):
        phase_section(section, rows_ref[section], first_ref, wide_ref, phase_ref)

    @pl.loop(0, NC)
    def _(c):
        column_step(c, second_ref, third_ref, fourth_ref, phase_ref, spec_ref, mix_ref, acc_ref)

    for pair in range(2 * PR):
        flow_rows, flow_cols = finish_pair(pair, acc_ref, sums_ref)
        distance, node_row = divmod(pair, PR)
        out_ref[distance, 0, node_row : node_row + 1] = flow_rows
        out_ref[distance, 1, node_row : node_row + 1] = flow_cols


def raw_flows(rows, interpret=False):
    return pl.pallas_call(
        flow_kernel,
        out_shape=jax.ShapeDtypeStruct((2, 2, PR, NC), jnp.float32),
        in_specs=[pl.BlockSpec(memory_space=pltpu.VMEM)] * 6,
        out_specs=pl.BlockSpec(memory_space=pltpu.VMEM),
        scratch_shapes=[
            pltpu.VMEM((PR * 2 * FOLD, WIDE), jnp.float32),
            pltpu.VMEM((2, 3 * PR * 2 * FOLD, WIDE), jnp.bfloat16),
            pltpu.VMEM((3 * PR * 2 * FOLD, 256), jnp.float32),
            pltpu.VMEM((2 * PR, 2 * FOLD, 256), jnp.bfloat16),
            pltpu.VMEM((3, 2 * PR, NC, 8, P_SIZE), jnp.float32),
        ],
        compiler_params=pltpu.CompilerParams(vmem_limit_bytes=40 * 1024 * 1024),
        cost_estimate=pl.CostEstimate(
            flops=10**10, bytes_accessed=4 * 10**6, transcendentals=1700000
        ),
        interpret=interpret,
    )(rows, *[jnp.asarray(table) for table in folded_tables()])


def from_behind(block, axis, distance):
    devices = range(lax.axis_size(axis))
    route = [(i - distance, i) for i in devices if i - distance in devices]
    return lax.ppermute(block, axis, route)


def frame_strips(stack):
    low = from_behind(stack, "tile", 1)
    high = from_behind(stack[:, :ABOVE], "tile", -1)
    return jnp.concatenate([low, stack, high], axis=1)


def per_device(images, patch_mask, springs, groups):
    strip = images[0]
    own_mask = patch_mask[0]
    strips = [strip] + [from_behind(strip, "sec", distance) for distance in (1, 2)]
    masks = [from_behind(own_mask, "sec", distance) for distance in (1, 2)]
    raw = raw_flows(frame_strips(jnp.stack(strips)))
    section = lax.axis_index("sec")
    own_float = own_mask.astype(jnp.float32)
    weights = []
    for distance in (1, 2):
        earlier = jnp.maximum(section - distance, 0)
        linked = ((groups[section] == groups[earlier]) & (section >= distance)).astype(jnp.float32)
        weights.append(own_float * masks[distance - 1].astype(jnp.float32) * linked)
    weights = jnp.stack(weights)
    flows = raw * weights[:, None]
    global_rows = PR * lax.axis_index("tile") + jnp.arange(PR, dtype=jnp.int32)
    last_row = PR * lax.axis_size("tile") - 1
    col_ids = jnp.arange(NC, dtype=jnp.int32)
    down = springs[0, 0].astype(jnp.float32) * (global_rows < last_row).astype(jnp.float32)[:, None]
    right = springs[0, 1].astype(jnp.float32) * (col_ids < NC - 1).astype(jnp.float32)[None, :]
    payload = jnp.concatenate([flows.reshape(4, PR, NC), weights, down[None], right[None]])
    reach = RELAX // PR
    around = jnp.concatenate(
        [
            payload if far == 0 else from_behind(payload, "tile", -far)
            for far in range(-reach, reach + 1)
        ],
        axis=1,
    )
    pull = around[0:2] + around[2:4]
    near = around[4] + around[5]
    moved = pull / jnp.maximum(near, 1.0)
    down = around[6]
    right = around[7]
    up = jnp.pad(down, ((1, 0), (0, 0)))[:-1]
    left = jnp.pad(right, ((0, 0), (1, 0)))[:, :-1]
    for sweep in range(RELAX):
        framed = jnp.pad(moved, ((0, 0), (1, 1), (1, 1)))
        force = spring_stiffness * (
            down * (framed[:, 2:, 1:-1] - moved)
            + up * (framed[:, :-2, 1:-1] - moved)
            + right * (framed[:, 1:-1, 2:] - moved)
            + left * (framed[:, 1:-1, :-2] - moved)
        )
        force = force + flow_pull * (pull - near * moved)
        moved = moved + step_size * force
    moved = moved[:, RELAX : RELAX + PR]
    return (flows[None], moved[None])


def solution(mesh):
    return jax.shard_map(
        per_device,
        mesh=mesh,
        in_specs=(
            P("sec", "tile", None),
            P("sec", "tile", None),
            P("sec", None, "tile", None),
            P(),
        ),
        out_specs=(P("sec", None, None, "tile", None), P("sec", None, "tile", None)),
        check_vma=False,
    )
```

profile of v0, /device:TPU:0, one launch (start us, length us, event | category | flops | bytes accessed | tf_op | source)
XLA Modules:
  0.0 63.9 jit_solution(6158211918048273107)
XLA Ops:
  0.7 5.0 %collective-permute-start.1 = (bf16[80,760]{1,0:T(8,128)(2,1)}, bf16[80,760]{1,0:T(8,128)(2,1)S(1)}, u32[]{:S(2)}, u32[]{:S(2)}) collective-permute-start(bf16[80,760]{1,0:T(8,128)(2,1)} %bitcast.33), channel_id=1, source_target_pairs={{0,16},{8,24},{1,17},{9,25},{2,18},{10,26},{3,19},{11,27},{4,20},{... | collective-permute-start | bytes 364808 | tf_op jit(solution)/shard_map/ppermute | solution.py:198
  5.7 3.4 %collective-permute-start = (bf16[80,760]{1,0:T(8,128)(2,1)}, bf16[80,760]{1,0:T(8,128)(2,1)S(1)}, u32[]{:S(2)}, u32[]{:S(2)}) collective-permute-start(bf16[80,760]{1,0:T(8,128)(2,1)} %bitcast.34), channel_id=1, source_target_pairs={{0,8},{8,16},{16,24},{1,9},{9,17},{17,25},{2,10},{10,18},{18,26},{... | collective-permute-start | bytes 364808 | tf_op jit(solution)/shard_map/ppermute | solution.py:198
  9.1 1.9 %collective-permute-start.4 = (s32[2,16]{1,0:T(2,128)}, s32[2,16]{1,0:T(2,128)S(1)}, u32[]{:S(2)}, u32[]{:S(2)}) collective-permute-start(s32[2,16]{1,0:T(2,128)} %bitcast.40), channel_id=1, source_target_pairs={{0,8},{8,16},{16,24},{1,9},{9,17},{17,25},{2,10},{10,18},{18,26},{... | collective-permute-start | bytes 392 | tf_op jit(solution)/shard_map/ppermute | solution.py:198
  11.0 1.3 %collective-permute-start.5 = (s32[2,16]{1,0:T(2,128)}, s32[2,16]{1,0:T(2,128)S(1)}, u32[]{:S(2)}, u32[]{:S(2)}) collective-permute-start(s32[2,16]{1,0:T(2,128)} %bitcast.41), channel_id=1, source_target_pairs={{0,16},{8,24},{1,17},{9,25},{2,18},{10,26},{3,19},{11,27},{4,20},{... | collective-permute-start | bytes 392 | tf_op jit(solution)/shard_map/ppermute | solution.py:198
  12.3 0.9 %pad_maximum_fusion.1 = bf16[3,80,760]{2,1,0:T(8,128)(2,1)S(1)} fusion(bf16[1,80,760]{2,1,0:T(8,128)(2,1)S(1)} %bitcast.35, bf16[1,80,760]{2,1,0:T(8,128)(2,1)S(1)} %bitcast.37, bf16[1,80,760]{2,1,0:T(8,128)(2,1)} %param.9), kind=kLoop, calls=%fused_computation.1 | loop fusion | flops 364800 | bytes 729600 | tf_op jit(solution)/shard_map/stack | solution.py:212
  13.3 1.3 %collective-permute-start.2 = (bf16[3,80,760]{2,1,0:T(8,128)(2,1)S(1)}, bf16[3,80,760]{2,1,0:T(8,128)(2,1)S(1)}, u32[]{:S(2)}, u32[]{:S(2)}) collective-permute-start(bf16[3,80,760]{2,1,0:T(8,128)(2,1)S(1)} %pad_maximum_fusion.1), channel_id=1, source_target_pairs={{0,1},{1,2},{2,3},{3,4},{4,5},{5,6},{6,7},{8,9},{9,10},{10,11},{11... | collective-permute-start | bytes 1094408 | tf_op jit(solution)/shard_map/ppermute | solution.py:198
  14.6 1.4 %fusion.24 = (s32[1]{0:T(128)}, s32[1]{0:T(128)}, s32[1]{0:T(128)}) fusion(s32[4]{0:T(128)} %param.12, s32[]{:T(128)S(6)} %max.13, s32[]{:T(128)S(6)} %select_n.2, s32[]{:T(128)S(6)} %max.14), kind=kLoop, calls=%fused_computation.64 | loop fusion | bytes 36 | tf_op jit(solution)/shard_map/dynamic_slice | solution.py:218
  18.7 1.4 %collective-permute-start.3 = (bf16[3,48,760]{2,1,0:T(8,128)(2,1)S(1)}, bf16[3,48,760]{2,1,0:T(8,128)(2,1)S(1)}, u32[]{:S(2)}, u32[]{:S(2)}) collective-permute-start(bf16[3,48,760]{2,1,0:T(8,128)(2,1)S(1)} %slice.112), channel_id=1, source_target_pairs={{1,0},{2,1},{3,2},{4,3},{5,4},{6,5},{7,6},{9,8},{10,9},{11,10},{12... | collective-permute-start | bytes 656648 | tf_op jit(solution)/shard_map/ppermute | solution.py:198
  20.2 3.8 %collective-permute-done.3 = bf16[3,48,760]{2,1,0:T(8,128)(2,1)S(1)} collective-permute-done((bf16[3,48,760]{2,1,0:T(8,128)(2,1)S(1)}, bf16[3,48,760]{2,1,0:T(8,128)(2,1)S(1)}, u32[]{:S(2)}, u32[]{:S(2)}) %collective-permute-start.3) | collective-permute-done | bytes 218912 | tf_op jit(solution)/shard_map/ppermute | solution.py:198
  24.0 0.1 pad_maximum_fusion.rows_ref
  24.2 21.8 %shard_map.104 = f32[2,2,2,16]{3,2,1,0:T(2,128)S(1)} custom-call(bf16[3,208,760]{2,1,0:T(8,128)(2,1)S(1)} %pad_maximum_fusion.rows_ref, bf16[384,208]{1,0:T(8,128)(2,1)S(1)} %copy-done.1, bf16[8,256,256]{2,1,0:T(8,128)(2,1)S(1)} %copy-done, bf16[160,192]{1,0:T(8,128)(2,1)S(1)} %copy-done.3, bf16[256,160]{1,0:T(8,128)(2,1)S(1)} %copy-done.2, ...), custom_call_target="tpu_custom_call" | custom-call | flops 10000000000 | bytes 4000000 | tf_op jit(solution)/shard_map/pallas_call | solution.py:175
  46.0 0.1 constant_dynamic-update-slice_fusion.1
  46.1 6.0 %collective-permute-start.6 = (f32[8,2,16]{2,1,0:T(2,128)S(1)}, f32[8,2,16]{2,1,0:T(2,128)S(1)}, u32[]{:S(2)}, u32[]{:S(2)}) collective-permute-start(f32[8,2,16]{2,1,0:T(2,128)S(1)} %constant_dynamic-update-slice_fusion), channel_id=1, source_target_pairs={{0,2},{1,3},{2,4},{3,5},{4,6},{5,7},{8,10},{9,11},{10,12},{11,13},... | collective-permute-start | bytes 3080 | tf_op jit(solution)/shard_map/ppermute | solution.py:198
  52.1 3.5 %collective-permute-start.7 = (f32[8,2,16]{2,1,0:T(2,128)S(1)}, f32[8,2,16]{2,1,0:T(2,128)S(1)}, u32[]{:S(2)}, u32[]{:S(2)}) collective-permute-start(f32[8,2,16]{2,1,0:T(2,128)S(1)} %constant_dynamic-update-slice_fusion), channel_id=1, source_target_pairs={{0,1},{1,2},{2,3},{3,4},{4,5},{5,6},{6,7},{8,9},{9,10},{10,11},{11... | collective-permute-start | bytes 3080 | tf_op jit(solution)/shard_map/ppermute | solution.py:198
  55.6 1.3 %collective-permute-start.8 = (f32[8,2,16]{2,1,0:T(2,128)S(1)}, f32[8,2,16]{2,1,0:T(2,128)S(1)}, u32[]{:S(2)}, u32[]{:S(2)}) collective-permute-start(f32[8,2,16]{2,1,0:T(2,128)S(1)} %constant_dynamic-update-slice_fusion), channel_id=1, source_target_pairs={{1,0},{2,1},{3,2},{4,3},{5,4},{6,5},{7,6},{9,8},{10,9},{11,10},{12... | collective-permute-start | bytes 3080 | tf_op jit(solution)/shard_map/ppermute | solution.py:198
  56.9 1.3 %collective-permute-start.9 = (f32[8,2,16]{2,1,0:T(2,128)S(1)}, f32[8,2,16]{2,1,0:T(2,128)S(1)}, u32[]{:S(2)}, u32[]{:S(2)}) collective-permute-start(f32[8,2,16]{2,1,0:T(2,128)S(1)} %constant_dynamic-update-slice_fusion), channel_id=1, source_target_pairs={{2,0},{3,1},{4,2},{5,3},{6,4},{7,5},{10,8},{11,9},{12,10},{13,11},... | collective-permute-start | bytes 3080 | tf_op jit(solution)/shard_map/ppermute | solution.py:198
  58.2 0.6 fusion.25
  58.8 4.0 %collective-permute-done.9 = f32[8,2,16]{2,1,0:T(2,128)S(1)} collective-permute-done((f32[8,2,16]{2,1,0:T(2,128)S(1)}, f32[8,2,16]{2,1,0:T(2,128)S(1)}, u32[]{:S(2)}, u32[]{:S(2)}) %collective-permute-start.9) | collective-permute-done | bytes 1056 | tf_op jit(solution)/shard_map/ppermute | solution.py:198
  62.9 0.1 pad_slice_fusion.7
  63.0 0.1 multiply_add_fusion.2
  63.1 0.1 multiply_add_fusion.1
  63.2 0.1 multiply_add_fusion
  63.2 0.1 subtract_multiply_fusion.1
  63.3 0.6 fusion.23
  (40 shorter events, 0.2 us)
Async XLA Ops:
  0.6 23.4 %copy-start.5 = (bf16[1,80,760]{2,1,0:T(8,128)(2,1)S(1)}, bf16[1,80,760]{2,1,0:T(8,128)(2,1)}, u32[]{:S(2)}) copy-start(bf16[1,80,760]{2,1,0:T(8,128)(2,1)} %param.9) | copy-start | bytes 364804
  0.6 19.5 %copy-start.7 = (s32[1,2,16]{2,1,0:T(2,128)S(1)}, s32[1,2,16]{2,1,0:T(2,128)}, u32[]{:S(2)}) copy-start(s32[1,2,16]{2,1,0:T(2,128)} %param.10) | copy-start | bytes 388
  0.7 11.7 %collective-permute-start.1 = (bf16[80,760]{1,0:T(8,128)(2,1)}, bf16[80,760]{1,0:T(8,128)(2,1)S(1)}, u32[]{:S(2)}, u32[]{:S(2)}) collective-permute-start(bf16[80,760]{1,0:T(8,128)(2,1)} %bitcast.33), channel_id=1, source_target_pairs={{0,16},{8,24},{1,17},{9,25},{2,18},{10,26},{3,19},{11,27},{4,20},{... | collective-permute-start | bytes 364808 | tf_op jit(solution)/shard_map/ppermute | solution.py:198
  5.7 6.7 %collective-permute-start = (bf16[80,760]{1,0:T(8,128)(2,1)}, bf16[80,760]{1,0:T(8,128)(2,1)S(1)}, u32[]{:S(2)}, u32[]{:S(2)}) collective-permute-start(bf16[80,760]{1,0:T(8,128)(2,1)} %bitcast.34), channel_id=1, source_target_pairs={{0,8},{8,16},{16,24},{1,9},{9,17},{17,25},{2,10},{10,18},{18,26},{... | collective-permute-start | bytes 364808 | tf_op jit(solution)/shard_map/ppermute | solution.py:198
  9.1 11.1 %collective-permute-start.4 = (s32[2,16]{1,0:T(2,128)}, s32[2,16]{1,0:T(2,128)S(1)}, u32[]{:S(2)}, u32[]{:S(2)}) collective-permute-start(s32[2,16]{1,0:T(2,128)} %bitcast.40), channel_id=1, source_target_pairs={{0,8},{8,16},{16,24},{1,9},{9,17},{17,25},{2,10},{10,18},{18,26},{... | collective-permute-start | bytes 392 | tf_op jit(solution)/shard_map/ppermute | solution.py:198
  11.0 9.2 %collective-permute-start.5 = (s32[2,16]{1,0:T(2,128)}, s32[2,16]{1,0:T(2,128)S(1)}, u32[]{:S(2)}, u32[]{:S(2)}) collective-permute-start(s32[2,16]{1,0:T(2,128)} %bitcast.41), channel_id=1, source_target_pairs={{0,16},{8,24},{1,17},{9,25},{2,18},{10,26},{3,19},{11,27},{4,20},{... | collective-permute-start | bytes 392 | tf_op jit(solution)/shard_map/ppermute | solution.py:198
  13.3 10.7 %collective-permute-start.2 = (bf16[3,80,760]{2,1,0:T(8,128)(2,1)S(1)}, bf16[3,80,760]{2,1,0:T(8,128)(2,1)S(1)}, u32[]{:S(2)}, u32[]{:S(2)}) collective-permute-start(bf16[3,80,760]{2,1,0:T(8,128)(2,1)S(1)} %pad_maximum_fusion.1), channel_id=1, source_target_pairs={{0,1},{1,2},{2,3},{3,4},{4,5},{5,6},{6,7},{8,9},{9,10},{10,11},{11... | collective-permute-start | bytes 1094408 | tf_op jit(solution)/shard_map/ppermute | solution.py:198
  18.7 5.5 %copy-start = (bf16[8,256,256]{2,1,0:T(8,128)(2,1)S(1)}, bf16[8,256,256]{2,1,0:T(8,128)(2,1)}, u32[]{:S(2)}) copy-start(bf16[8,256,256]{2,1,0:T(8,128)(2,1)} %constant.44.clone.second_ref) | copy-start | bytes 3145732
  18.7 5.5 %copy-start.1 = (bf16[384,208]{1,0:T(8,128)(2,1)S(1)}, bf16[384,208]{1,0:T(8,128)(2,1)}, u32[]{:S(2)}) copy-start(bf16[384,208]{1,0:T(8,128)(2,1)} %constant.43.clone.first_ref) | copy-start | bytes 479236
  18.7 5.5 %copy-start.2 = (bf16[256,160]{1,0:T(8,128)(2,1)S(1)}, bf16[256,160]{1,0:T(8,128)(2,1)}, u32[]{:S(2)}) copy-start(bf16[256,160]{1,0:T(8,128)(2,1)} %constant.46.clone.fourth_ref) | copy-start | bytes 245764
  18.7 5.5 %copy-start.3 = (bf16[160,192]{1,0:T(8,128)(2,1)S(1)}, bf16[160,192]{1,0:T(8,128)(2,1)}, u32[]{:S(2)}) copy-start(bf16[160,192]{1,0:T(8,128)(2,1)} %constant.45.clone.third_ref) | copy-start | bytes 184324
  18.7 5.4 %copy-start.4 = (f32[8,160]{1,0:T(8,128)S(1)}, f32[8,160]{1,0:T(8,128)}, u32[]{:S(2)}) copy-start(f32[8,160]{1,0:T(8,128)} %constant.47.clone.sums_ref) | copy-start | bytes 15364
  18.7 5.3 %collective-permute-start.3 = (bf16[3,48,760]{2,1,0:T(8,128)(2,1)S(1)}, bf16[3,48,760]{2,1,0:T(8,128)(2,1)S(1)}, u32[]{:S(2)}, u32[]{:S(2)}) collective-permute-start(bf16[3,48,760]{2,1,0:T(8,128)(2,1)S(1)} %slice.112), channel_id=1, source_target_pairs={{1,0},{2,1},{3,2},{4,3},{5,4},{6,5},{7,6},{9,8},{10,9},{11,10},{12... | collective-permute-start | bytes 656648 | tf_op jit(solution)/shard_map/ppermute | solution.py:198
  24.2 21.9 %copy-start.6 = (s32[1,2,2,16]{3,2,1,0:T(2,128)S(1)}, s32[1,2,2,16]{3,2,1,0:T(2,128)}, u32[]{:S(2)}) copy-start(s32[1,2,2,16]{3,2,1,0:T(2,128)} %param.11) | copy-start | bytes 772
  46.1 12.7 %collective-permute-start.6 = (f32[8,2,16]{2,1,0:T(2,128)S(1)}, f32[8,2,16]{2,1,0:T(2,128)S(1)}, u32[]{:S(2)}, u32[]{:S(2)}) collective-permute-start(f32[8,2,16]{2,1,0:T(2,128)S(1)} %constant_dynamic-update-slice_fusion), channel_id=1, source_target_pairs={{0,2},{1,3},{2,4},{3,5},{4,6},{5,7},{8,10},{9,11},{10,12},{11,13},... | collective-permute-start | bytes 3080 | tf_op jit(solution)/shard_map/ppermute | solution.py:198
  52.1 6.7 %collective-permute-start.7 = (f32[8,2,16]{2,1,0:T(2,128)S(1)}, f32[8,2,16]{2,1,0:T(2,128)S(1)}, u32[]{:S(2)}, u32[]{:S(2)}) collective-permute-start(f32[8,2,16]{2,1,0:T(2,128)S(1)} %constant_dynamic-update-slice_fusion), channel_id=1, source_target_pairs={{0,1},{1,2},{2,3},{3,4},{4,5},{5,6},{6,7},{8,9},{9,10},{10,11},{11... | collective-permute-start | bytes 3080 | tf_op jit(solution)/shard_map/ppermute | solution.py:198
  55.6 3.2 %collective-permute-start.8 = (f32[8,2,16]{2,1,0:T(2,128)S(1)}, f32[8,2,16]{2,1,0:T(2,128)S(1)}, u32[]{:S(2)}, u32[]{:S(2)}) collective-permute-start(f32[8,2,16]{2,1,0:T(2,128)S(1)} %constant_dynamic-update-slice_fusion), channel_id=1, source_target_pairs={{1,0},{2,1},{3,2},{4,3},{5,4},{6,5},{7,6},{9,8},{10,9},{11,10},{12... | collective-permute-start | bytes 3080 | tf_op jit(solution)/shard_map/ppermute | solution.py:198
  56.9 5.9 %collective-permute-start.9 = (f32[8,2,16]{2,1,0:T(2,128)S(1)}, f32[8,2,16]{2,1,0:T(2,128)S(1)}, u32[]{:S(2)}, u32[]{:S(2)}) collective-permute-start(f32[8,2,16]{2,1,0:T(2,128)S(1)} %constant_dynamic-update-slice_fusion), channel_id=1, source_target_pairs={{2,0},{3,1},{4,2},{5,3},{6,4},{7,5},{10,8},{11,9},{12,10},{13,11},... | collective-permute-start | bytes 3080 | tf_op jit(solution)/shard_map/ppermute | solution.py:198
where the time goes:
time: 64.3 us; the launch traced here: 63.9 us
  starting transfers between devices  26.4 us (41%)
  Pallas kernels  21.8 us (34%)
  waiting for transfers between devices  7.81 us (12%)
  between operations  3.56 us (6%)
  other arithmetic  2.71 us (4%)
  local copies, waits for them, and re-layouts  1.66 us (3%)
    ppermute x10, starting transfers between devices, from_behind(): return lax.ppermute(block, axis, route)  26.4 us
    pallas_call x1, Pallas kernels, raw_flows(): pl.pallas_call(flow_kernel, out_shape=jax.ShapeDtypeStruct((2, 2, PR, NC)...  21.8 us
    ppermute x10, waiting for transfers between devices, from_behind(): return lax.ppermute(block, axis, route)  7.81 us
    dynamic_slice x1, local copies, waits for them, and re-layouts, per_device(): groups[earlier]  1.43 us
  transfers between devices with their start and end apart: 10, of which 2 were waited for; matrix products, arithmetic and copies ran while one was open for 5% of the time, Pallas kernels for 0%

commit v1 on v0

v1 whole, which is shorter than its diff:
```python
import functools
import math

import jax
import jax.numpy as jnp
import numpy as np
from jax import lax
from jax.experimental import pallas as pl
from jax.experimental.pallas import tpu as pltpu
from jax.sharding import PartitionSpec as P

P_SIZE = 160
STRIDE = 40
PR = 2
NC = 16
RELAX = 4
HALF = 80
ABOVE = 48
ROWS = 2 * HALF + ABOVE
FOLD = 96
WIDE = 768
SHIFT = 64
TILES = P_SIZE // 8
SLOTS = 2 * RELAX // PR + 1
KINDS = 5

spring_stiffness = 1.0
flow_pull = 0.5
step_size = 0.2
sharpness = 25.0


def full_tables():
    indices = np.arange(P_SIZE)
    angle = (indices[:, None] * indices[None, :] % P_SIZE).astype(np.float32) * np.float32(
        2.0 * math.pi / P_SIZE
    )
    exact = angle.astype(np.float64)
    cosine = np.cos(exact).astype(np.float32).astype(jnp.bfloat16).astype(np.float32)
    sine = np.sin(exact).astype(np.float32).astype(jnp.bfloat16).astype(np.float32)
    return cosine, sine


def folded_tables():
    cosine, sine = full_tables()
    kept = HALF + 1
    first = np.zeros((PR, 2, FOLD, ROWS), np.float32)
    for node_row in range(PR):
        rows = slice(node_row * STRIDE, node_row * STRIDE + P_SIZE)
        first[node_row, 0, :kept, rows] = cosine[:kept]
        first[node_row, 1, :kept, rows] = sine[:kept]
    second = np.zeros((8, 256, 256), np.float32)
    for case in range(8):
        offset = STRIDE * case % SHIFT
        second[case, offset : offset + P_SIZE, :kept] = cosine[:, :kept]
        second[case, offset : offset + P_SIZE, 128 : 128 + kept] = sine[:, :kept]
    twice = np.full((kept,), 2.0, np.float32)
    twice[0] = twice[HALF] = 1.0
    third = np.zeros((P_SIZE, 2 * FOLD), np.float32)
    third[:, :kept] = cosine[:, :kept] * twice
    third[:, FOLD : FOLD + kept] = -2.0 * sine[:, :kept]
    fourth = np.zeros((256, P_SIZE), np.float32)
    fourth[:kept] = cosine[:kept] * twice[:, None]
    fourth[128 : 128 + kept] = -2.0 * sine[:kept]
    offsets = (np.arange(P_SIZE) + HALF) % P_SIZE - HALF
    sums = np.zeros((8, P_SIZE), np.float32)
    sums[0] = 1.0
    sums[1] = offsets
    made = [
        table.astype(jnp.bfloat16)
        for table in (first.reshape(PR * 2 * FOLD, ROWS), second, third, fourth)
    ]
    return made + [sums]


def dot(left, right):
    return jnp.dot(left, right, preferred_element_type=jnp.float32)


def phase_section(section, rows, first_ref, wide_ref, phase_ref):
    wide_ref[:, : rows.shape[1]] = dot(first_ref[...], rows)
    whole = wide_ref[...]
    phase_ref[section, 0] = whole.astype(jnp.bfloat16)
    phase_ref[section, 1] = pltpu.roll(whole, WIDE - SHIFT, 1).astype(jnp.bfloat16)


def column_spectrum(c, section, phase_ref, second_ref):
    block = STRIDE * c // SHIFT
    start = pl.multiple_of(block // 2 * 128, 128)
    window = phase_ref[section, block % 2, :, pl.ds(start, 256)]
    return dot(window, second_ref[c % 8])


def quarters(ref, node_row):
    low = node_row * 2 * FOLD
    return (
        ref[low : low + FOLD, :128],
        ref[low + FOLD : low + 2 * FOLD, 128:],
        ref[low + FOLD : low + 2 * FOLD, :128],
        ref[low : low + FOLD, 128:],
    )


def column_step(c, distance, own_ref, spec_ref, mix_ref, acc_ref, third_ref, fourth_ref):
    factor = sharpness / float(P_SIZE) ** 4 * math.log2(math.e)
    for node_row in range(PR):
        p, q, u, v = quarters(own_ref.at[c], node_row)
        pp, qq, uu, vv = quarters(spec_ref, node_row)
        mix_ref[node_row, :FOLD, :128] = (p * pp + q * qq + u * uu + v * vv).astype(jnp.bfloat16)
        mix_ref[node_row, :FOLD, 128:] = (u * qq - v * pp + p * vv - q * uu).astype(jnp.bfloat16)
        mix_ref[node_row, FOLD:, :128] = (p * uu - u * pp + v * qq - q * vv).astype(jnp.bfloat16)
        mix_ref[node_row, FOLD:, 128:] = (p * qq + q * pp - u * vv - v * uu).astype(jnp.bfloat16)
    for node_row in range(PR):
        pair = (distance - 1) * PR + node_row
        back = dot(third_ref[...], mix_ref[node_row]).astype(jnp.bfloat16)
        raw = dot(back, fourth_ref[...])
        pieces = [raw[8 * i : 8 * i + 8] for i in range(TILES)]
        top = functools.reduce(jnp.maximum, pieces)
        total = jnp.zeros_like(top)
        lean = jnp.zeros_like(top)
        for i, piece in enumerate(pieces):
            weight = jnp.exp2((piece - top) * factor)
            total = total + weight
            base = float(8 * i if 8 * i < HALF else 8 * i - P_SIZE)
            if base:
                lean = lean + base * weight
        acc_ref[0, pair, c] = top
        acc_ref[1, pair, c] = total
        acc_ref[2, pair, c] = lean


def finish_pair(pair, acc_ref, sums_ref):
    factor = sharpness / float(P_SIZE) ** 4 * math.log2(math.e)
    tops = acc_ref[0, pair]
    top = jnp.max(jnp.max(tops, axis=2, keepdims=True), axis=1, keepdims=True)
    scale = jnp.exp2((tops - top) * factor)
    total = acc_ref[1, pair] * scale
    within = lax.broadcasted_iota(jnp.int32, total.shape, 1).astype(jnp.float32)
    lean = acc_ref[2, pair] * scale + within * total
    total = jnp.sum(total, axis=1)
    lean = jnp.sum(lean, axis=1)

    def over_lanes(values):
        return lax.dot_general(
            sums_ref[...],
            values,
            (((1,), (1,)), ((), ())),
            precision=lax.Precision.HIGHEST,
            preferred_element_type=jnp.float32,
        )

    sums = over_lanes(total)
    leans = over_lanes(lean)
    return leans[0:1] / sums[0:1], sums[1:2] / sums[0:1]


def relax(pay_ref, field_ref, out_ref):
    field_ref[...] = jnp.zeros_like(field_ref)
    for slot in range(SLOTS):
        for kind in range(KINDS):
            field_ref[kind, PR * slot : PR * slot + PR] = pay_ref[
                slot, PR * kind : PR * kind + PR
            ]
    near = field_ref[2]
    down = field_ref[3]
    right = field_ref[4]
    rows = down.shape[0]
    up = pltpu.roll(down, 1, 0)
    left = pltpu.roll(right, 1, 1)
    for part in range(2):
        pull = field_ref[part]
        moved = pull / jnp.maximum(near, 1.0)
        for sweep in range(RELAX):
            force = spring_stiffness * (
                down * (pltpu.roll(moved, rows - 1, 0) - moved)
                + up * (pltpu.roll(moved, 1, 0) - moved)
                + right * (pltpu.roll(moved, 127, 1) - moved)
                + left * (pltpu.roll(moved, 1, 1) - moved)
            )
            force = force + flow_pull * (pull - near * moved)
            moved = moved + step_size * force
        out_ref[part] = moved[RELAX : RELAX + PR, :NC]


def mesh_kernel(
    sections, tiles,
    groups_ref, strip_ref, mask_ref, springs_ref, first_ref, third_ref, fourth_ref, sums_ref,
    second_hbm,
    flows_ref, moved_ref,
    rows_ref, masks_ref, pay_ref, second_ref, wide_ref, phase_ref, own_ref, spec_ref, mix_ref,
    acc_ref, field_ref, send_sem, recv_sem, table_sem,
):
    sec = lax.axis_index("sec")
    tile = lax.axis_index("tile")
    fill = pltpu.make_async_copy(second_hbm, second_ref, table_sem)
    fill.start()

    pay_ref[...] = jnp.zeros_like(pay_ref)
    barrier = pltpu.get_barrier_semaphore()
    expected = 0
    for axis, here, size in (("sec", sec, sections), ("tile", tile, tiles)):
        for far in (-2, -1, 1, 2):
            there = here + far
            present = (there >= 0) & (there < size)

            @pl.when(present)
            def _():
                pl.semaphore_signal(
                    barrier, inc=1, device_id={axis: there}, device_id_type=pl.DeviceIdType.MESH
                )

            expected = expected + present.astype(jnp.int32)

    for distance in (1, 2):

        @pl.when(sec < distance)
        def _():
            rows_ref[distance] = jnp.zeros(rows_ref.shape[1:], rows_ref.dtype)
            masks_ref[distance - 1] = jnp.zeros(masks_ref.shape[1:], masks_ref.dtype)

    @pl.when(tile == 0)
    def _():
        rows_ref[:, :HALF] = jnp.zeros((3, HALF, rows_ref.shape[2]), rows_ref.dtype)

    @pl.when(tile == tiles - 1)
    def _():
        rows_ref[:, 2 * HALF :] = jnp.zeros((3, ABOVE, rows_ref.shape[2]), rows_ref.dtype)

    wide_ref[:, WIDE - 128 :] = jnp.zeros((wide_ref.shape[0], 128), jnp.float32)
    pl.semaphore_wait(barrier, expected)

    class Hop:
        def __init__(self, number, source, target, axis, far, held=None):
            here, size = (sec, sections) if axis == "sec" else (tile, tiles)
            self.sends = (here + far >= 0) & (here + far < size)
            self.gets = (here - far >= 0) & (here - far < size)
            if held is not None:
                self.sends = self.sends & held
                self.gets = self.gets & held
            self.copy = pltpu.make_async_remote_copy(
                src_ref=source,
                dst_ref=target,
                send_sem=send_sem.at[number],
                recv_sem=recv_sem.at[number],
                device_id={axis: here + far},
                device_id_type=pl.DeviceIdType.MESH,
            )

        def start(self):
            pl.when(self.sends)(self.copy.start)

        def arrive(self):
            pl.when(self.gets)(self.copy.wait_recv)

        def finish(self):
            pl.when(self.sends)(self.copy.wait_send)

    across = [
        Hop(k, strip_ref, rows_ref.at[k + 1, pl.ds(HALF, HALF)], "sec", k + 1) for k in range(2)
    ]
    marks = [Hop(2 + k, mask_ref, masks_ref.at[k], "sec", k + 1) for k in range(2)]
    beside = []
    for k in range(3):
        held = None if k == 0 else sec >= k
        whole = strip_ref if k == 0 else rows_ref.at[k, pl.ds(HALF, HALF)]
        edge = strip_ref.at[pl.ds(0, ABOVE)] if k == 0 else rows_ref.at[k, pl.ds(HALF, ABOVE)]
        beside.append(
            [
                Hop(4 + 2 * k, whole, rows_ref.at[k, pl.ds(0, HALF)], "tile", 1, held),
                Hop(5 + 2 * k, edge, rows_ref.at[k, pl.ds(2 * HALF, ABOVE)], "tile", -1, held),
            ]
        )
    middle = SLOTS // 2
    spread = [
        Hop(10 + i, pay_ref.at[middle], pay_ref.at[middle - far], "tile", far)
        for i, far in enumerate((-1, 1, -2, 2))
    ]
    for hop in across + beside[0] + marks:
        hop.start()
    rows_ref[0, HALF : 2 * HALF] = strip_ref[...]
    across[0].arrive()
    for hop in beside[1]:
        hop.start()
    for hop in beside[0]:
        hop.arrive()
    phase_section(0, rows_ref[0], first_ref, wide_ref, phase_ref)
    fill.wait()
    across[1].arrive()
    for hop in beside[2]:
        hop.start()

    @pl.loop(0, NC)
    def _(c):
        own_ref[c] = column_spectrum(c, 0, phase_ref, second_ref)

    for distance in (1, 2):
        for hop in beside[distance]:
            hop.arrive()
        phase_section(distance, rows_ref[distance], first_ref, wide_ref, phase_ref)

        @pl.loop(0, NC)
        def _(c):
            spec_ref[...] = column_spectrum(c, distance, phase_ref, second_ref)
            column_step(
                c, distance, own_ref, spec_ref, mix_ref, acc_ref, third_ref, fourth_ref
            )

    for hop in marks:
        hop.arrive()
    own_mask = mask_ref[...].astype(jnp.float32)
    pulls = [[0.0, 0.0], [0.0, 0.0]]
    near = jnp.zeros((PR, NC), jnp.float32)
    for distance in (1, 2):
        earlier = jnp.maximum(sec - distance, 0)
        linked = (groups_ref[sec] == groups_ref[earlier]) & (sec >= distance)
        weight = own_mask * masks_ref[distance - 1].astype(jnp.float32)
        weight = weight * jnp.where(linked, 1.0, 0.0)
        near = near + weight
        for node_row in range(PR):
            found = finish_pair((distance - 1) * PR + node_row, acc_ref, sums_ref)
            for part in range(2):
                flow = found[part] * weight[node_row : node_row + 1]
                flows_ref[distance - 1, part, node_row : node_row + 1] = flow
                pulls[part][node_row] = pulls[part][node_row] + flow
    for part in range(2):
        for node_row in range(PR):
            at = PR * part + node_row
            pay_ref[middle, at : at + 1, :NC] = pulls[part][node_row]
    pay_ref[middle, 2 * PR : 3 * PR, :NC] = near
    global_rows = PR * tile + lax.broadcasted_iota(jnp.int32, (PR, NC), 0)
    col_ids = lax.broadcasted_iota(jnp.int32, (PR, NC), 1)
    pay_ref[middle, 3 * PR : 4 * PR, :NC] = jnp.where(
        global_rows < PR * tiles - 1, springs_ref[0].astype(jnp.float32), 0.0
    )
    pay_ref[middle, 4 * PR : 5 * PR, :NC] = jnp.where(
        col_ids < NC - 1, springs_ref[1].astype(jnp.float32), 0.0
    )
    for hop in spread:
        hop.start()
    for hop in spread:
        hop.arrive()
    relax(pay_ref, field_ref, moved_ref)
    for hop in across + marks + beside[0] + beside[1] + beside[2] + spread:
        hop.finish()


def per_device(images, patch_mask, springs, groups):
    sections, tiles = lax.axis_size("sec"), lax.axis_size("tile")
    first, second, third, fourth, sums = [jnp.asarray(table) for table in folded_tables()]
    strip = images[0]
    span = PR * 2 * FOLD
    vmem = pl.BlockSpec(memory_space=pltpu.VMEM)
    flows, moved = pl.pallas_call(
        functools.partial(mesh_kernel, sections, tiles),
        out_shape=(
            jax.ShapeDtypeStruct((2, 2, PR, NC), jnp.float32),
            jax.ShapeDtypeStruct((2, PR, NC), jnp.float32),
        ),
        in_specs=[pl.BlockSpec(memory_space=pltpu.SMEM)]
        + [vmem] * 7
        + [pl.BlockSpec(memory_space=pl.ANY)],
        out_specs=(vmem, vmem),
        scratch_shapes=[
            pltpu.VMEM((3, ROWS, strip.shape[1]), jnp.bfloat16),
            pltpu.VMEM((2, PR, NC), jnp.int32),
            pltpu.VMEM((SLOTS, 16, 128), jnp.float32),
            pltpu.VMEM(second.shape, jnp.bfloat16),
            pltpu.VMEM((span, WIDE), jnp.float32),
            pltpu.VMEM((3, 2, span, WIDE), jnp.bfloat16),
            pltpu.VMEM((NC, span, 256), jnp.float32),
            pltpu.VMEM((span, 256), jnp.float32),
            pltpu.VMEM((PR, 2 * FOLD, 256), jnp.bfloat16),
            pltpu.VMEM((3, 2 * PR, NC, 8, P_SIZE), jnp.float32),
            pltpu.VMEM((KINDS, 16, 128), jnp.float32),
            pltpu.SemaphoreType.DMA((14,)),
            pltpu.SemaphoreType.DMA((14,)),
            pltpu.SemaphoreType.DMA,
        ],
        compiler_params=pltpu.CompilerParams(
            vmem_limit_bytes=48 * 1024 * 1024, collective_id=0, has_side_effects=True
        ),
        cost_estimate=pl.CostEstimate(
            flops=10**10, bytes_accessed=4 * 10**6, transcendentals=1700000
        ),
    )(groups, strip, patch_mask[0], springs[0], first, third, fourth, sums, second)
    return (flows[None], moved[None])


def solution(mesh):
    return jax.shard_map(
        per_device,
        mesh=mesh,
        in_specs=(
            P("sec", "tile", None),
            P("sec", "tile", None),
            P("sec", None, "tile", None),
            P(),
        ),
        out_specs=(P("sec", None, None, "tile", None), P("sec", None, "tile", None)),
        check_vma=False,
    )
```

time: 64.3 us -> 49.5 us (0.77)
  the two profiles are of different devices: /device:TPU:0 before, /device:TPU:5 now
where the time goes in v1:
time: 49.5 us; the launch traced here: 49.1 us
  Pallas kernels  41.8 us (84%)
  local copies, waits for them, and re-layouts  6.7 us (14%)
  between operations  0.68 us (1%)
    pallas_call x1, Pallas kernels, per_device(): pl.pallas_call(functools.partial(mesh_kernel, sections, tiles), out_shape...  41.8 us
    unnamed x20, local copies, waits for them, and re-layouts  6.7 us

profile of v1, /device:TPU:5, one launch (start us, length us, event | category | flops | bytes accessed | tf_op | source)
XLA Modules:
  0.0 49.1 jit_solution(5724105293136311537)
XLA Ops:
  0.6 0.0 copy-start.8
  0.6 0.0 copy-start.1
  0.7 0.0 copy-start.2
  0.7 0.0 copy-start.3
  0.7 0.7 %copy-done.8 = f32[8,160]{1,0:T(8,128)S(1)} copy-done((f32[8,160]{1,0:T(8,128)S(1)}, f32[8,160]{1,0:T(8,128)}, u32[]{:S(2)}) %copy-start.8) | copy-done | bytes 5144
  1.3 0.0 copy-done.1
  1.3 0.0 copy-done.2
  1.3 0.0 copy-done.3
  1.3 0.0 copy-start
  1.3 0.9 %copy-done = bf16[1,80,760]{2,1,0:T(8,128)(2,1)S(1)} copy-done((bf16[1,80,760]{2,1,0:T(8,128)(2,1)S(1)}, bf16[1,80,760]{2,1,0:T(8,128)(2,1)}, u32[]{:S(2)}) %copy-start) | copy-done | bytes 121624
  2.2 0.0 copy-start.4
  2.3 1.2 %copy-done.4 = bf16[8,256,256]{2,1,0:T(8,128)(2,1)S(1)} copy-done((bf16[8,256,256]{2,1,0:T(8,128)(2,1)S(1)}, bf16[8,256,256]{2,1,0:T(8,128)(2,1)}, u32[]{:S(2)}) %copy-start.4) | copy-done | bytes 1048600
  3.5 0.0 copy-start.5
  3.5 0.9 %copy-done.5 = bf16[384,208]{1,0:T(8,128)(2,1)S(1)} copy-done((bf16[384,208]{1,0:T(8,128)(2,1)S(1)}, bf16[384,208]{1,0:T(8,128)(2,1)}, u32[]{:S(2)}) %copy-start.5) | copy-done | bytes 159768
  4.4 0.0 copy-start.6
  4.4 0.9 %copy-done.6 = bf16[256,160]{1,0:T(8,128)(2,1)S(1)} copy-done((bf16[256,160]{1,0:T(8,128)(2,1)S(1)}, bf16[256,160]{1,0:T(8,128)(2,1)}, u32[]{:S(2)}) %copy-start.6) | copy-done | bytes 81944
  5.3 0.0 copy-start.7
  5.3 0.9 %copy-done.7 = bf16[160,192]{1,0:T(8,128)(2,1)S(1)} copy-done((bf16[160,192]{1,0:T(8,128)(2,1)S(1)}, bf16[160,192]{1,0:T(8,128)(2,1)}, u32[]{:S(2)}) %copy-start.7) | copy-done | bytes 61464
  6.2 41.8 %shard_map.104 = (f32[2,2,2,16]{3,2,1,0:T(2,128)S(1)}, f32[2,2,16]{2,1,0:T(2,128)S(1)}) custom-call(s32[4]{0:T(128)S(1)} %copy-done.3, bf16[80,760]{1,0:T(8,128)(2,1)S(1)} %bitcast.7, s32[2,16]{1,0:T(2,128)S(1)} %bitcast.9, s32[2,2,16]{2,1,0:T(2,128)S(1)} %bitcast.8, bf16[384,208]{1,0:T(8,128)(2,1)S(1)} %copy-done.5, bf16[160,192]{1,0:T(8,128)(2,1)S(1)} %copy-done.7, ...), custom_call_target="tpu_custom_call" | custom-call | flops 10000000000 | bytes 4000000 | tf_op jit(solution)/shard_map/pallas_call | solution.py:353
  48.0 0.6 %copy.13 = f32[1,2,2,2,16]{4,3,2,1,0:T(2,128)} copy(f32[1,2,2,2,16]{4,3,2,1,0:T(2,128)S(1)} %bitcast.5) | data formatting | bytes 1024
  48.6 0.6 %copy.14 = f32[1,2,2,16]{3,2,1,0:T(2,128)} copy(f32[1,2,2,16]{3,2,1,0:T(2,128)S(1)} %bitcast.6) | data formatting | bytes 512
Async XLA Ops:
  0.6 0.7 %copy-start.8 = (f32[8,160]{1,0:T(8,128)S(1)}, f32[8,160]{1,0:T(8,128)}, u32[]{:S(2)}) copy-start(f32[8,160]{1,0:T(8,128)} %constant.14.clone.sums_ref) | copy-start | bytes 15364
  0.6 0.7 %copy-start.1 = (s32[1,2,2,16]{3,2,1,0:T(2,128)S(1)}, s32[1,2,2,16]{3,2,1,0:T(2,128)}, u32[]{:S(2)}) copy-start(s32[1,2,2,16]{3,2,1,0:T(2,128)} %param.11) | copy-start | bytes 772
  0.7 0.7 %copy-start.2 = (s32[1,2,16]{2,1,0:T(2,128)S(1)}, s32[1,2,16]{2,1,0:T(2,128)}, u32[]{:S(2)}) copy-start(s32[1,2,16]{2,1,0:T(2,128)} %param.10) | copy-start | bytes 388
  0.7 0.7 %copy-start.3 = (s32[4]{0:T(128)S(1)}, s32[4]{0:T(128)}, u32[]{:S(2)}) copy-start(s32[4]{0:T(128)} %groups_ref.1) | copy-start | bytes 52
  1.3 0.9 %copy-start = (bf16[1,80,760]{2,1,0:T(8,128)(2,1)S(1)}, bf16[1,80,760]{2,1,0:T(8,128)(2,1)}, u32[]{:S(2)}) copy-start(bf16[1,80,760]{2,1,0:T(8,128)(2,1)} %param.9) | copy-start | bytes 364804
  2.2 1.2 %copy-start.4 = (bf16[8,256,256]{2,1,0:T(8,128)(2,1)S(1)}, bf16[8,256,256]{2,1,0:T(8,128)(2,1)}, u32[]{:S(2)}) copy-start(bf16[8,256,256]{2,1,0:T(8,128)(2,1)} %constant.11.clone.second_hbm) | copy-start | bytes 3145732
  3.5 0.9 %copy-start.5 = (bf16[384,208]{1,0:T(8,128)(2,1)S(1)}, bf16[384,208]{1,0:T(8,128)(2,1)}, u32[]{:S(2)}) copy-start(bf16[384,208]{1,0:T(8,128)(2,1)} %constant.10.clone.first_ref) | copy-start | bytes 479236
  4.4 0.9 %copy-start.6 = (bf16[256,160]{1,0:T(8,128)(2,1)S(1)}, bf16[256,160]{1,0:T(8,128)(2,1)}, u32[]{:S(2)}) copy-start(bf16[256,160]{1,0:T(8,128)(2,1)} %constant.13.clone.fourth_ref) | copy-start | bytes 245764
  5.3 0.9 %copy-start.7 = (bf16[160,192]{1,0:T(8,128)(2,1)S(1)}, bf16[160,192]{1,0:T(8,128)(2,1)}, u32[]{:S(2)}) copy-start(bf16[160,192]{1,0:T(8,128)(2,1)} %constant.12.clone.third_ref) | copy-start | bytes 184324

commit v2 on v1

--- a/solution.py
+++ b/solution.py
@@ -84,11 +84,11 @@
     phase_ref[section, 1] = pltpu.roll(whole, WIDE - SHIFT, 1).astype(jnp.bfloat16)
 
 
-def column_spectrum(c, section, phase_ref, second_ref):
+def column_spectrum(c, section, phase_ref, second_ref, case):
     block = STRIDE * c // SHIFT
     start = pl.multiple_of(block // 2 * 128, 128)
     window = phase_ref[section, block % 2, :, pl.ds(start, 256)]
-    return dot(window, second_ref[c % 8])
+    return dot(window, second_ref[case])
 
 
 def quarters(ref, node_row):
@@ -101,32 +101,43 @@
     )
 
 
-def column_step(c, distance, own_ref, spec_ref, mix_ref, acc_ref, third_ref, fourth_ref):
+def cross_step(low, own, spec, mix):
+    p, q, u, v = quarters(own, low)
+    pp, qq, uu, vv = quarters(spec, low)
+    mix[:FOLD, :128] = (p * pp + q * qq + u * uu + v * vv).astype(jnp.bfloat16)
+    mix[:FOLD, 128:] = (u * qq - v * pp + p * vv - q * uu).astype(jnp.bfloat16)
+    mix[FOLD:, :128] = (p * uu - u * pp + v * qq - q * vv).astype(jnp.bfloat16)
+    mix[FOLD:, 128:] = (p * qq + q * pp - u * vv - v * uu).astype(jnp.bfloat16)
+
+
+def peak_step(raw, pair, c, acc_ref):
     factor = sharpness / float(P_SIZE) ** 4 * math.log2(math.e)
-    for node_row in range(PR):
-        p, q, u, v = quarters(own_ref.at[c], node_row)
-        pp, qq, uu, vv = quarters(spec_ref, node_row)
-        mix_ref[node_row, :FOLD, :128] = (p * pp + q * qq + u * uu + v * vv).astype(jnp.bfloat16)
-        mix_ref[node_row, :FOLD, 128:] = (u * qq - v * pp + p * vv - q * uu).astype(jnp.bfloat16)
-        mix_ref[node_row, FOLD:, :128] = (p * uu - u * pp + v * qq - q * vv).astype(jnp.bfloat16)
-        mix_ref[node_row, FOLD:, 128:] = (p * qq + q * pp - u * vv - v * uu).astype(jnp.bfloat16)
-    for node_row in range(PR):
+    pieces = [raw[8 * i : 8 * i + 8] for i in range(TILES)]
+    top = functools.reduce(jnp.maximum, pieces)
+    total = jnp.zeros_like(top)
+    lean = jnp.zeros_like(top)
+    for i, piece in enumerate(pieces):
+        weight = jnp.exp2((piece - top) * factor)
+        total = total + weight
+        base = float(8 * i if 8 * i < HALF else 8 * i - P_SIZE)
+        if base:
+            lean = lean + base * weight
+    acc_ref[0, pair, c] = top
+    acc_ref[1, pair, c] = total
+    acc_ref[2, pair, c] = lean
+
+
+def column_steps(c, distance, own_ref, spec_ref, mix_ref, back_ref, acc_ref, third_ref, fourth_ref):
+    both = [(half, node_row) for half in range(2) for node_row in range(PR)]
+    for i, (half, node_row) in enumerate(both):
+        cross_step(node_row, own_ref.at[c + 8 * half], spec_ref.at[half], mix_ref.at[i])
+    for i in range(len(both)):
+        back = dot(third_ref[...], mix_ref[i])
+        back_ref[i * P_SIZE : (i + 1) * P_SIZE] = back.astype(jnp.bfloat16)
+    raw = dot(back_ref[...], fourth_ref[...])
+    for i, (half, node_row) in enumerate(both):
         pair = (distance - 1) * PR + node_row
-        back = dot(third_ref[...], mix_ref[node_row]).astype(jnp.bfloat16)
-        raw = dot(back, fourth_ref[...])
-        pieces = [raw[8 * i : 8 * i + 8] for i in range(TILES)]
-        top = functools.reduce(jnp.maximum, pieces)
-        total = jnp.zeros_like(top)
-        lean = jnp.zeros_like(top)
-        for i, piece in enumerate(pieces):
-            weight = jnp.exp2((piece - top) * factor)
-            total = total + weight
-            base = float(8 * i if 8 * i < HALF else 8 * i - P_SIZE)
-            if base:
-                lean = lean + base * weight
-        acc_ref[0, pair, c] = top
-        acc_ref[1, pair, c] = total
-        acc_ref[2, pair, c] = lean
+        peak_step(raw[i * P_SIZE : (i + 1) * P_SIZE], pair, c + 8 * half, acc_ref)
 
 
 def finish_pair(pair, acc_ref, sums_ref):
@@ -184,16 +195,31 @@
 
 def mesh_kernel(
     sections, tiles,
-    groups_ref, strip_ref, mask_ref, springs_ref, first_ref, third_ref, fourth_ref, sums_ref,
-    second_hbm,
+    groups_ref, strip_ref, mask_hbm, springs_hbm, first_hbm, second_hbm, third_hbm, fourth_hbm,
+    sums_hbm,
     flows_ref, moved_ref,
-    rows_ref, masks_ref, pay_ref, second_ref, wide_ref, phase_ref, own_ref, spec_ref, mix_ref,
-    acc_ref, field_ref, send_sem, recv_sem, table_sem,
+    mask_ref, springs_ref, first_ref, second_ref, third_ref, fourth_ref, sums_ref,
+    rows_ref, masks_ref, pay_ref, wide_ref, phase_ref, own_ref, spec_ref, mix_ref,
+    back_ref, acc_ref, field_ref, send_sem, recv_sem, table_sem,
 ):
     sec = lax.axis_index("sec")
     tile = lax.axis_index("tile")
-    fill = pltpu.make_async_copy(second_hbm, second_ref, table_sem)
-    fill.start()
+    fetched = (
+        (strip_ref, rows_ref.at[0, pl.ds(HALF, HALF)]),
+        (first_hbm, first_ref),
+        (second_hbm, second_ref),
+        (third_hbm, third_ref),
+        (fourth_hbm, fourth_ref),
+        (sums_hbm, sums_ref),
+        (mask_hbm, mask_ref),
+        (springs_hbm, springs_ref),
+    )
+    fetches = [
+        pltpu.make_async_copy(source, target, table_sem.at[i])
+        for i, (source, target) in enumerate(fetched)
+    ]
+    for fetch in fetches:
+        fetch.start()
 
     pay_ref[...] = jnp.zeros_like(pay_ref)
     barrier = pltpu.get_barrier_semaphore()
@@ -258,7 +284,7 @@
     across = [
         Hop(k, strip_ref, rows_ref.at[k + 1, pl.ds(HALF, HALF)], "sec", k + 1) for k in range(2)
     ]
-    marks = [Hop(2 + k, mask_ref, masks_ref.at[k], "sec", k + 1) for k in range(2)]
+    marks = [Hop(2 + k, mask_hbm, masks_ref.at[k], "sec", k + 1) for k in range(2)]
     beside = []
     for k in range(3):
         held = None if k == 0 else sec >= k
@@ -277,32 +303,34 @@
     ]
     for hop in across + beside[0] + marks:
         hop.start()
-    rows_ref[0, HALF : 2 * HALF] = strip_ref[...]
+    for fetch in fetches:
+        fetch.wait()
     across[0].arrive()
     for hop in beside[1]:
         hop.start()
     for hop in beside[0]:
         hop.arrive()
     phase_section(0, rows_ref[0], first_ref, wide_ref, phase_ref)
-    fill.wait()
     across[1].arrive()
     for hop in beside[2]:
         hop.start()
 
-    @pl.loop(0, NC)
+    @pl.loop(0, NC // 2)
     def _(c):
-        own_ref[c] = column_spectrum(c, 0, phase_ref, second_ref)
+        for half in range(2):
+            own_ref[c + 8 * half] = column_spectrum(c + 8 * half, 0, phase_ref, second_ref, c)
 
     for distance in (1, 2):
         for hop in beside[distance]:
             hop.arrive()
         phase_section(distance, rows_ref[distance], first_ref, wide_ref, phase_ref)
 
-        @pl.loop(0, NC)
+        @pl.loop(0, NC // 2)
         def _(c):
-            spec_ref[...] = column_spectrum(c, distance, phase_ref, second_ref)
-            column_step(
-                c, distance, own_ref, spec_ref, mix_ref, acc_ref, third_ref, fourth_ref
+            for half in range(2):
+                spec_ref[half] = column_spectrum(c + 8 * half, distance, phase_ref, second_ref, c)
+            column_steps(
+                c, distance, own_ref, spec_ref, mix_ref, back_ref, acc_ref, third_ref, fourth_ref
             )
 
     for hop in marks:
@@ -357,32 +385,38 @@
             jax.ShapeDtypeStruct((2, PR, NC), jnp.float32),
         ),
         in_specs=[pl.BlockSpec(memory_space=pltpu.SMEM)]
-        + [vmem] * 7
-        + [pl.BlockSpec(memory_space=pl.ANY)],
+        + [pl.BlockSpec(memory_space=pl.ANY)] * 8,
         out_specs=(vmem, vmem),
         scratch_shapes=[
+            pltpu.VMEM((PR, NC), jnp.int32),
+            pltpu.VMEM((2, PR, NC), jnp.int32),
+            pltpu.VMEM(first.shape, jnp.bfloat16),
+            pltpu.VMEM(second.shape, jnp.bfloat16),
+            pltpu.VMEM(third.shape, jnp.bfloat16),
+            pltpu.VMEM(fourth.shape, jnp.bfloat16),
+            pltpu.VMEM(sums.shape, jnp.float32),
             pltpu.VMEM((3, ROWS, strip.shape[1]), jnp.bfloat16),
             pltpu.VMEM((2, PR, NC), jnp.int32),
             pltpu.VMEM((SLOTS, 16, 128), jnp.float32),
-            pltpu.VMEM(second.shape, jnp.bfloat16),
             pltpu.VMEM((span, WIDE), jnp.float32),
             pltpu.VMEM((3, 2, span, WIDE), jnp.bfloat16),
             pltpu.VMEM((NC, span, 256), jnp.float32),
-            pltpu.VMEM((span, 256), jnp.float32),
-            pltpu.VMEM((PR, 2 * FOLD, 256), jnp.bfloat16),
+            pltpu.VMEM((2, span, 256), jnp.float32),
+            pltpu.VMEM((2 * PR, 2 * FOLD, 256), jnp.bfloat16),
+            pltpu.VMEM((2 * PR * P_SIZE, 256), jnp.bfloat16),
             pltpu.VMEM((3, 2 * PR, NC, 8, P_SIZE), jnp.float32),
             pltpu.VMEM((KINDS, 16, 128), jnp.float32),
             pltpu.SemaphoreType.DMA((14,)),
             pltpu.SemaphoreType.DMA((14,)),
-            pltpu.SemaphoreType.DMA,
+            pltpu.SemaphoreType.DMA((8,)),
         ],
         compiler_params=pltpu.CompilerParams(
-            vmem_limit_bytes=48 * 1024 * 1024, collective_id=0, has_side_effects=True
+            vmem_limit_bytes=60 * 1024 * 1024, collective_id=0, has_side_effects=True
         ),
         cost_estimate=pl.CostEstimate(
             flops=10**10, bytes_accessed=4 * 10**6, transcendentals=1700000
         ),
-    )(groups, strip, patch_mask[0], springs[0], first, third, fourth, sums, second)
+    )(groups, strip, patch_mask[0], springs[0], first, second, third, fourth, sums)
     return (flows[None], moved[None])
 
 

time: 49.5 us -> 34.2 us (0.69)
  Pallas kernels: 41.8 us -> 31.4 us
  local copies, waits for them, and re-layouts: 6.7 us -> 1.91 us
    pallas_call x1, Pallas kernels: 41.8 us -> 31.4 us  [per_device(): pl.pallas_call(functools.partial(mesh_kernel, sections, tiles), out_shape...]
    unnamed x20 -> x6, local copies, waits for them, and re-layouts: 6.7 us -> 1.91 us
where the time goes in v2:
time: 34.2 us; the launch traced here: 34 us
  Pallas kernels  31.4 us (92%)
  local copies, waits for them, and re-layouts  1.91 us (6%)
  between operations  0.65 us (2%)
    pallas_call x1, Pallas kernels, per_device(): pl.pallas_call(functools.partial(mesh_kernel, sections, tiles), out_shape...  31.4 us
    unnamed x6, local copies, waits for them, and re-layouts  1.91 us

profile of v2, /device:TPU:5, one launch (start us, length us, event | category | flops | bytes accessed | tf_op | source)
XLA Modules:
  0.0 34.0 jit_solution(16689690092493800169)
XLA Ops:
  0.6 31.4 %shard_map.104 = (f32[2,2,2,16]{3,2,1,0:T(2,128)}, f32[2,2,16]{2,1,0:T(2,128)}) custom-call(s32[4]{0:T(128)} %groups_ref.1, bf16[80,760]{1,0:T(8,128)(2,1)} %bitcast.7, s32[2,16]{1,0:T(2,128)} %bitcast.9, s32[2,2,16]{2,1,0:T(2,128)} %bitcast.8, bf16[384,208]{1,0:T(8,128)(2,1)} %constant.10.clone.first_hbm, bf16[8,256,256]{2,1,0:T(8,128)(2,1)} %constant.11.clone.second_hbm, ...), custom_call_target="tpu_custom_call" | custom-call | flops 10000000000 | bytes 4000000 | tf_op jit(solution)/shard_map/pallas_call | solution.py:381
  32.0 0.0 copy-start
  32.0 0.7 %copy-done = f32[2,2,2,16]{3,2,1,0:T(2,128)S(1)} copy-done((f32[2,2,2,16]{3,2,1,0:T(2,128)S(1)}, f32[2,2,2,16]{3,2,1,0:T(2,128)}, u32[]{:S(2)}) %copy-start) | copy-done | bytes 536
  32.7 0.0 copy-start.1
  32.7 0.6 %copy.13 = f32[1,2,2,2,16]{4,3,2,1,0:T(2,128)} copy(f32[1,2,2,2,16]{4,3,2,1,0:T(2,128)S(1)} %bitcast.5) | data formatting | bytes 1024
  33.3 0.1 copy-done.1
  33.4 0.6 %copy.14 = f32[1,2,2,16]{3,2,1,0:T(2,128)} copy(f32[1,2,2,16]{3,2,1,0:T(2,128)S(1)} %bitcast.6) | data formatting | bytes 512
Async XLA Ops:
  32.0 0.7 %copy-start = (f32[2,2,2,16]{3,2,1,0:T(2,128)S(1)}, f32[2,2,2,16]{3,2,1,0:T(2,128)}, u32[]{:S(2)}) copy-start(f32[2,2,2,16]{3,2,1,0:T(2,128)} %get-tuple-element.4) | copy-start | bytes 1540
  32.7 0.7 %copy-start.1 = (f32[2,2,16]{2,1,0:T(2,128)S(1)}, f32[2,2,16]{2,1,0:T(2,128)}, u32[]{:S(2)}) copy-start(f32[2,2,16]{2,1,0:T(2,128)} %get-tuple-element.5) | copy-start | bytes 772

commit v3 on v2

--- a/solution.py
+++ b/solution.py
@@ -127,17 +127,24 @@
     acc_ref[2, pair, c] = lean
 
 
-def column_steps(c, distance, own_ref, spec_ref, mix_ref, back_ref, acc_ref, third_ref, fourth_ref):
-    both = [(half, node_row) for half in range(2) for node_row in range(PR)]
-    for i, (half, node_row) in enumerate(both):
+def cross_steps(c, own_ref, spec_ref, mix_ref):
+    for i in range(2 * PR):
+        half, node_row = divmod(i, PR)
         cross_step(node_row, own_ref.at[c + 8 * half], spec_ref.at[half], mix_ref.at[i])
-    for i in range(len(both)):
+
+
+def column_steps(mix_ref, back_ref, raw_ref, third_ref, fourth_ref):
+    for i in range(2 * PR):
         back = dot(third_ref[...], mix_ref[i])
         back_ref[i * P_SIZE : (i + 1) * P_SIZE] = back.astype(jnp.bfloat16)
-    raw = dot(back_ref[...], fourth_ref[...])
-    for i, (half, node_row) in enumerate(both):
+    raw_ref[...] = dot(back_ref[...], fourth_ref[...])
+
+
+def peak_steps(c, distance, raw_ref, acc_ref):
+    for i in range(2 * PR):
+        half, node_row = divmod(i, PR)
         pair = (distance - 1) * PR + node_row
-        peak_step(raw[i * P_SIZE : (i + 1) * P_SIZE], pair, c + 8 * half, acc_ref)
+        peak_step(raw_ref[i * P_SIZE : (i + 1) * P_SIZE], pair, c + 8 * half, acc_ref)
 
 
 def finish_pair(pair, acc_ref, sums_ref):
@@ -200,7 +207,7 @@
     flows_ref, moved_ref,
     mask_ref, springs_ref, first_ref, second_ref, third_ref, fourth_ref, sums_ref,
     rows_ref, masks_ref, pay_ref, wide_ref, phase_ref, own_ref, spec_ref, mix_ref,
-    back_ref, acc_ref, field_ref, send_sem, recv_sem, table_sem,
+    back_ref, raw_ref, acc_ref, field_ref, send_sem, recv_sem, table_sem,
 ):
     sec = lax.axis_index("sec")
     tile = lax.axis_index("tile")
@@ -252,6 +259,7 @@
     def _():
         rows_ref[:, 2 * HALF :] = jnp.zeros((3, ABOVE, rows_ref.shape[2]), rows_ref.dtype)
 
+    raw_ref[...] = jnp.zeros_like(raw_ref)
     wide_ref[:, WIDE - 128 :] = jnp.zeros((wide_ref.shape[0], 128), jnp.float32)
     pl.semaphore_wait(barrier, expected)
 
@@ -311,27 +319,35 @@
     for hop in beside[0]:
         hop.arrive()
     phase_section(0, rows_ref[0], first_ref, wide_ref, phase_ref)
-    across[1].arrive()
-    for hop in beside[2]:
-        hop.start()
 
     @pl.loop(0, NC // 2)
     def _(c):
         for half in range(2):
             own_ref[c + 8 * half] = column_spectrum(c + 8 * half, 0, phase_ref, second_ref, c)
 
+    across[1].arrive()
+    for hop in beside[2]:
+        hop.start()
+
     for distance in (1, 2):
         for hop in beside[distance]:
             hop.arrive()
         phase_section(distance, rows_ref[distance], first_ref, wide_ref, phase_ref)
+        for half in range(2):
+            spec_ref[half] = column_spectrum(8 * half, distance, phase_ref, second_ref, 0)
 
         @pl.loop(0, NC // 2)
         def _(c):
+            cross_steps(c, own_ref, spec_ref, mix_ref)
+            later = jnp.minimum(c + 1, NC // 2 - 1)
             for half in range(2):
-                spec_ref[half] = column_spectrum(c + 8 * half, distance, phase_ref, second_ref, c)
-            column_steps(
-                c, distance, own_ref, spec_ref, mix_ref, back_ref, acc_ref, third_ref, fourth_ref
-            )
+                spec_ref[half] = column_spectrum(
+                    later + 8 * half, distance, phase_ref, second_ref, later
+                )
+            peak_steps(jnp.maximum(c - 1, 0), distance, raw_ref, acc_ref)
+            column_steps(mix_ref, back_ref, raw_ref, third_ref, fourth_ref)
+
+        peak_steps(NC // 2 - 1, distance, raw_ref, acc_ref)
 
     for hop in marks:
         hop.arrive()
@@ -404,6 +420,7 @@
             pltpu.VMEM((2, span, 256), jnp.float32),
             pltpu.VMEM((2 * PR, 2 * FOLD, 256), jnp.bfloat16),
             pltpu.VMEM((2 * PR * P_SIZE, 256), jnp.bfloat16),
+            pltpu.VMEM((2 * PR * P_SIZE, P_SIZE), jnp.float32),
             pltpu.VMEM((3, 2 * PR, NC, 8, P_SIZE), jnp.float32),
             pltpu.VMEM((KINDS, 16, 128), jnp.float32),
             pltpu.SemaphoreType.DMA((14,)),

time: 34.2 us -> 29.9 us (0.87)
  Pallas kernels: 31.4 us -> 27.1 us
    pallas_call x1, Pallas kernels: 31.4 us -> 27.1 us  [per_device(): pl.pallas_call(functools.partial(mesh_kernel, sections, tiles), out_shape...]
where the time goes in v3:
time: 29.9 us; the launch traced here: 29.7 us
  Pallas kernels  27.1 us (91%)
  local copies, waits for them, and re-layouts  1.91 us (6%)
  between operations  0.65 us (2%)
    pallas_call x1, Pallas kernels, per_device(): pl.pallas_call(functools.partial(mesh_kernel, sections, tiles), out_shape...  27.1 us
    unnamed x6, local copies, waits for them, and re-layouts  1.91 us

profile of v3, /device:TPU:5, one launch (start us, length us, event | category | flops | bytes accessed | tf_op | source)
XLA Modules:
  0.0 29.7 jit_solution(17146830699482819362)
XLA Ops:
  0.6 27.1 %shard_map.104 = (f32[2,2,2,16]{3,2,1,0:T(2,128)}, f32[2,2,16]{2,1,0:T(2,128)}) custom-call(s32[4]{0:T(128)} %groups_ref.1, bf16[80,760]{1,0:T(8,128)(2,1)} %bitcast.7, s32[2,16]{1,0:T(2,128)} %bitcast.9, s32[2,2,16]{2,1,0:T(2,128)} %bitcast.8, bf16[384,208]{1,0:T(8,128)(2,1)} %constant.10.clone.first_hbm, bf16[8,256,256]{2,1,0:T(8,128)(2,1)} %constant.11.clone.second_hbm, ...), custom_call_target="tpu_custom_call" | custom-call | flops 10000000000 | bytes 4000000 | tf_op jit(solution)/shard_map/pallas_call | solution.py:397
  27.7 0.0 copy-start
  27.7 0.7 %copy-done = f32[2,2,2,16]{3,2,1,0:T(2,128)S(1)} copy-done((f32[2,2,2,16]{3,2,1,0:T(2,128)S(1)}, f32[2,2,2,16]{3,2,1,0:T(2,128)}, u32[]{:S(2)}) %copy-start) | copy-done | bytes 536
  28.4 0.0 copy-start.1
  28.4 0.6 %copy.13 = f32[1,2,2,2,16]{4,3,2,1,0:T(2,128)} copy(f32[1,2,2,2,16]{4,3,2,1,0:T(2,128)S(1)} %bitcast.5) | data formatting | bytes 1024
  29.0 0.1 copy-done.1
  29.1 0.6 %copy.14 = f32[1,2,2,16]{3,2,1,0:T(2,128)} copy(f32[1,2,2,16]{3,2,1,0:T(2,128)S(1)} %bitcast.6) | data formatting | bytes 512
Async XLA Ops:
  27.7 0.7 %copy-start = (f32[2,2,2,16]{3,2,1,0:T(2,128)S(1)}, f32[2,2,2,16]{3,2,1,0:T(2,128)}, u32[]{:S(2)}) copy-start(f32[2,2,2,16]{3,2,1,0:T(2,128)} %get-tuple-element.4) | copy-start | bytes 1540
  28.4 0.7 %copy-start.1 = (f32[2,2,16]{2,1,0:T(2,128)S(1)}, f32[2,2,16]{2,1,0:T(2,128)}, u32[]{:S(2)}) copy-start(f32[2,2,16]{2,1,0:T(2,128)} %get-tuple-element.5) | copy-start | bytes 772
